TPU v7x, 128 devices: a whole 4x4x4 slice. The times are simulated.
128 devices in a mesh: dp: 16 (over y, x_lo, core), blk: 8 (over z, x_hi).
Axes of the slice: x: 4 (x_hi: 2, x_lo: 2; x = x_hi * 2 + x_lo), y: 4, z: 4, core: 2. Of those that a mesh axis runs over, the one named last changes fastest.
Arguments:
- tokens: bfloat16 [8, 512, 5120], P('blk'), may hold values from -6 to 6
- cotangent: bfloat16 [8, 512, 5120], P('blk'), may hold values from -0.119628906 to 0.119628906
- gain: float32 [5120], replicated, may hold values from 0.1 to 1.9
- up_weight: bfloat16 [13824, 5120], P(('dp', 'blk')), may hold values from -0.078125 to 0.078125
- down_weight: bfloat16 [13824, 5120], P(('dp', 'blk')), may hold values from -0.0546875 to 0.0546875
Outputs:
- block_out: bfloat16 [8, 512, 5120], P('blk', 'dp')
- grad_gain: float32 [5120], replicated
- grad_up: bfloat16 [13824, 5120], P(('dp', 'blk'))
- grad_down: bfloat16 [13824, 5120], P(('dp', 'blk'))
All inputs are finite; a program needn't handle non-finite values.
Results may differ from a plain program's by a relative error of at most 0.017.
Values may be sent and summed in bfloat16 or wider, within the bound.
A program may use at most 192 MiB of HBM per device.

v0:
```python
import jax
import jax.numpy as jnp
from jax import lax
from jax.sharding import PartitionSpec as P

D = 5120


def body(tokens, cotangent, gain, up_weight, down_weight):
    inputs = tokens[0].astype(jnp.float32)
    inverse_rms = lax.rsqrt(jnp.mean(inputs * inputs, axis=-1, keepdims=True) + 1e-05)
    unit_rows = inputs * inverse_rms
    normed = (unit_rows * gain).astype(jnp.bfloat16)
    up_all, down_all = (
        lax.all_gather(up_weight, "blk", axis=0, tiled=True),
        lax.all_gather(down_weight, "blk", axis=0, tiled=True),
    )
    hidden = jnp.einsum("td,fd->tf", normed, up_all, preferred_element_type=jnp.float32)
    active = jax.nn.silu(hidden).astype(jnp.bfloat16)
    share_rows = active.shape[0] // lax.axis_size("dp")
    out_share = lax.psum_scatter(
        jnp.dot(active, down_all, preferred_element_type=jnp.float32).astype(jnp.bfloat16),
        "dp",
        scatter_dimension=0,
        tiled=True,
    ).astype(jnp.float32)
    own_rows = lax.dynamic_slice_in_dim(inputs, lax.axis_index("dp") * share_rows, share_rows, 0)
    block_out = (own_rows + out_share).astype(jnp.bfloat16)[None]
    upstream = cotangent[0]
    back_grad = jnp.einsum("te,fe->tf", upstream, down_all, preferred_element_type=jnp.float32)
    sigmoid_h = jax.nn.sigmoid(hidden)
    hidden_grad = (back_grad * sigmoid_h * (1.0 + hidden * (1.0 - sigmoid_h))).astype(jnp.bfloat16)
    joined = lax.psum_scatter(
        jnp.concatenate(
            [
                jnp.einsum("tf,td->fd", hidden_grad, normed, preferred_element_type=jnp.float32),
                jnp.einsum("tf,td->fd", active, upstream, preferred_element_type=jnp.float32),
            ],
            axis=1,
        ).astype(jnp.bfloat16),
        "blk",
        scatter_dimension=0,
        tiled=True,
    ).astype(jnp.float32)
    up_summed = joined[:, :D]
    down_summed = joined[:, D:]
    normal_grad = jnp.dot(hidden_grad, up_all, preferred_element_type=jnp.float32)
    partial_gain = jnp.sum(normal_grad * unit_rows, axis=0)
    grad_gain = lax.psum(partial_gain, ("dp", "blk"))
    return (block_out, grad_gain, up_summed.astype(jnp.bfloat16), down_summed.astype(jnp.bfloat16))


def solution(mesh):
    placed = (
        P("blk", None, None),
        P("blk", None, None),
        P(),
        P(("dp", "blk"), None),
        P(("dp", "blk"), None),
    )
    return jax.shard_map(
        body,
        mesh=mesh,
        in_specs=placed,
        out_specs=(P("blk", "dp", None), P(), P(("dp", "blk"), None), P(("dp", "blk"), None)),
        check_vma=False,
    )
```

profile of v0, /device:TPU:0, one launch (start us, length us, event | category | flops | bytes accessed | tf_op | source)
XLA Modules:
  0.0 1034.5 jit_solution(12945861363848201219)
XLA Ops:
  7.2 0.7 all-gather.5.cloned.1.call-update
  7.9 0.0 all-gather.7.cloned.1.call-start
  7.9 0.7 all-gather.7.cloned.1.call-update
  8.6 0.0 reduce-scatter.2.cloned.1.call-start
  8.7 3.6 fusion
  12.3 114.9 %all-gather.5.cloned.1.call-done = bf16[8,108,5120]{2,1,0:T(8,128)(2,1)} async-done(((bf16[1,108,5120]{2,1,0:T(8,128)(2,1)}), bf16[8,108,5120]{2,1,0:T(8,128)(2,1)}) %all-gather.5.cloned.1.call-update) | async-done | bytes 8847376 | tf_op jit(solution)/shard_map/all_gather | solution.py:15
  127.2 8.0 reshape.20
  135.1 9.8 fusion.6
  145.0 96.6 %all-gather.7.cloned.1.call-done = bf16[8,108,5120]{2,1,0:T(8,128)(2,1)} async-done(((bf16[1,108,5120]{2,1,0:T(8,128)(2,1)}), bf16[8,108,5120]{2,1,0:T(8,128)(2,1)}) %all-gather.7.cloned.1.call-update) | async-done | bytes 8847376 | tf_op jit(solution)/shard_map/all_gather | solution.py:16
  241.6 7.9 reshape.22
  249.5 11.0 %convolution_convert_fusion.2 = bf16[512,5120]{1,0:T(8,128)(2,1)} fusion(bf16[864,5120]{1,0:T(8,128)(2,1)} %reshape.22, f32[512,864]{0,1:T(8,128)S(1)} %fusion.6), kind=kOutput, calls=%fused_computation.8 | convolution fusion | flops 4534681600 | bytes 15859712 | tf_op jit(solution)/shard_map/dot_general | solution.py:22
  260.6 0.2 all-reduce.3.cloned.1.call-start
  260.8 10.2 multiply_convert_fusion.1
  271.1 0.9 copy-done.3
  272.0 8.0 convolution_convert_fusion.1
  280.0 7.8 convolution_convert_fusion
  287.8 7.2 pad_maximum_fusion
  295.1 7.9 convert_element_type.28
  302.9 0.6 dynamic-slice.1
  304.2 11.2 %multiply_reduce_fusion = f32[5120]{0:T(1024)S(1)} fusion(bf16[512,864]{0,1:T(8,128)(2,1)S(1)} %copy-done.4, bf16[864,5120]{1,0:T(8,128)(2,1)} %reshape.20, bf16[1,512,5120]{2,1,0:T(8,128)(2,1)} %param.5, f32[512]{0:T(512)S(1)} %add_rsqrt_fusion), kind=kOutput, calls=%fused_computation.4 | convolution fusion | flops 4540328960 | bytes 14997504 | tf_op jit(solution)/shard_map/dot_general | solution.py:47
  315.3 366.3 %psum.7 = f32[5120]{0:T(1024)} all-reduce(f32[5120]{0:T(1024)S(1)} %multiply_reduce_fusion), channel_id=1, replica_groups=mesh['dp'=16,'blk'=8] {'dp','blk'}, use_global_device_ids=true, to_apply=%region_3.4 | all-reduce | flops 5120 | bytes 40960 | tf_op jit(solution)/shard_map/psum | solution.py:49
  681.7 2.0 fusion.8
  683.7 340.8 %all-reduce.3.cloned.1.call-done = bf16[864,10240]{1,0:T(8,128)(2,1)} async-done(((bf16[864,10240]{1,0:T(8,128)(2,1)}), bf16[864,10240]{1,0:T(8,128)(2,1)}) %all-reduce.3.cloned.1.call-update) | async-done | bytes 17694736
  1024.5 3.5 fusion.9
  (14 shorter events, 0.1 us)
Async XLA Ops:
  7.2 120.0 %all-gather.5.cloned.1.call-start = ((), (), s32[]{:S(2)}) async-start(), calls=%async_computation.2 | async-start | bytes 10321920 | tf_op jit(solution)/shard_map/all_gather | solution.py:15
  7.9 233.7 %all-gather.7.cloned.1.call-start = ((), (), s32[]{:S(2)}) async-start(), calls=%async_computation.3 | async-start | bytes 10321920 | tf_op jit(solution)/shard_map/all_gather | solution.py:16
  8.6 673.0 %reduce-scatter.2.cloned.1.call-start = ((), (), s32[]{:S(2)}) async-start(), calls=%async_computation.1 | async-start | bytes 5570560 | tf_op jit(solution)/shard_map/reduce_scatter | solution.py:21
  12.3 122.8 %copy-start = (f32[5120]{0:T(1024)S(1)}, f32[5120]{0:T(1024)}, u32[]{:S(2)}) copy-start(f32[5120]{0:T(1024)} %param.7) | copy-start | bytes 61444
  145.0 115.8 %copy-start.2 = (f32[512,864]{0,1:T(8,128)}, f32[512,864]{0,1:T(8,128)S(1)}, u32[]{:S(2)}) copy-start(f32[512,864]{0,1:T(8,128)S(1)} %fusion.6) | copy-start | bytes 5308420
  260.6 763.9 %all-reduce.3.cloned.1.call-start = ((), (), s32[]{:S(2)}) async-start(), calls=%async_computation.4 | async-start | bytes 35389440
  271.0 0.9 copy-start.3
  295.0 7.9 copy-start.1
  295.1 9.1 copy-start.4
Sparse Core Ops, SparseCore 0:
  10.3 116.8 all-gather.4
  129.5 112.1 all-gather.6
  260.7 70.8 reduce-scatter.1
  334.1 690.3 all-reduce.2
where the time goes:
time: 1040 us; the launch traced here: 1030 us
  waiting for transfers between devices  554 us (53%)
  blocking collectives  366 us (35%)
  matrix products  58.1 us (6%)
  local copies, waits for them, and re-layouts  20.9 us (2%)
  other arithmetic  20.6 us (2%)
  between operations  14.5 us (1%)
    psum x1, blocking collectives, body(): grad_gain = lax.psum(partial_gain, ('dp', 'blk'))  366 us
    unnamed x5, waiting for transfers between devices  342 us
    all_gather x1, waiting for transfers between devices, body(): lax.all_gather(up_weight, 'blk', axis=0, tiled=True)  115 us
    all_gather x1, waiting for transfers between devices, body(): lax.all_gather(down_weight, 'blk', axis=0, tiled=True)  96.6 us
  transfers between devices with their start and end apart: 4, of which 3 were waited for; matrix products, arithmetic and copies ran while one was open for 7% of the time, Pallas kernels for 0%

commit v1 on v0

v1 whole, which is shorter than its diff:
```python
import jax
import jax.numpy as jnp
from jax import lax
from jax.experimental import pallas as pl
from jax.experimental.pallas import tpu as pltpu
from jax.sharding import PartitionSpec as P

D = 5120
TOK = 512
OWN = 108
SENT = 112
PAD = 128
STEP = 512
HALF = D // 2
HALVES = ((0, HALF), (HALF, D))
MESH = pl.DeviceIdType.MESH
BF16 = jnp.bfloat16
F32 = jnp.float32


def columns(step, size=STEP):
    return pl.ds(pl.multiple_of(step * size, size), size)


def dot(a, b, over):
    return lax.dot_general(a, b, ((over[:1], over[1:]), ((), ())), preferred_element_type=F32)


def kernel(
    tokens_ref, cotangent_ref, gain_ref, up_ref, down_ref,
    out_ref, gain_out_ref, grad_up_ref, grad_down_ref,
    norm, cot, weights, act, act_t, hidden_t, acc, grads, mail, x_first, y_first, y_second, x_second,
    own_rows, gain_acc, gain_own, gain_slots, send_sem, recv_sem, local_sem, free_sem,
):
    dp, blk = lax.axis_index("dp"), lax.axis_index("blk")
    y, x_lo, core = dp // 4, (dp // 2) % 2, dp % 2
    z, x_hi = blk // 2, blk % 2
    x = 2 * x_hi + x_lo

    def chip(cx, cy, cz, cc):
        return (cy * 4 + (cx % 2) * 2 + cc, cz * 2 + cx // 2)

    def x_at(j):
        return chip((x + j) % 4, y, z, core)

    def y_at(j):
        return chip(x, (y + j) % 4, z, core)

    def z_at(j):
        return chip(x, y, (z + j) % 4, core)

    sibling = chip(x, y, z, 1 - core)
    across = chip(3 - x, y, z, core)
    beside = chip(x + 1 - 2 * x_lo, y, z, core)

    count = [0]

    def send(src, dst, device):
        at = count[0]
        count[0] += 1
        copy = pltpu.make_async_remote_copy(
            src_ref=src, dst_ref=dst, send_sem=send_sem.at[at], recv_sem=recv_sem.at[at], device_id=device, device_id_type=MESH
        )
        copy.start()
        return copy

    load_tokens = pltpu.make_async_copy(tokens_ref.at[0], norm.at[0], local_sem.at[0])
    load_cot = pltpu.make_async_copy(cotangent_ref.at[0], cot.at[0], local_sem.at[1])
    load_own = pltpu.make_async_copy(tokens_ref.at[0, y, x_lo, core], own_rows, local_sem.at[2])
    load_tokens.start()
    load_cot.start()
    load_own.start()

    partners = [x_at(1), x_at(2), x_at(3), y_at(1), y_at(2), y_at(3), z_at(1), z_at(2), z_at(3), sibling]
    barrier = pltpu.get_barrier_semaphore()
    for partner in partners:
        pl.semaphore_signal(barrier, inc=1, device_id=partner, device_id_type=MESH)

    for kind, ref in enumerate((up_ref, down_ref)):
        weights[kind, 0, 96:PAD, :] = jnp.zeros((PAD - 96, D), BF16)
        weights[kind, 0, 0:OWN, :] = ref[...]
        for slot in range(1, 4):
            weights[kind, slot, SENT:PAD, :] = jnp.zeros((PAD - SENT, D), BF16)
    pl.semaphore_wait(barrier, len(partners))

    def block(kind, slot):
        return weights.at[kind, slot, pl.ds(0, SENT)]

    up_right = send(block(0, 0), block(0, 2), z_at(1))
    down_left = send(block(1, 0), block(1, 1), z_at(3))
    down_right = send(block(1, 0), block(1, 2), z_at(1))
    up_left = send(block(0, 0), block(0, 1), z_at(3))

    quarter = (y + 2 * x_lo) % 4
    quarter_across = (y + 2 - 2 * x_lo) % 4

    def piece(ref, which, q):
        return ref.at[which, q, :, core]

    load_cot.wait()
    cot_across = send(piece(cot, 0, quarter_across), piece(cot, 1, quarter_across), across)

    load_tokens.wait()
    gain = gain_ref[...]

    def normalize(step, _):
        at = (0, step // 8, (step // 4) % 2, (step // 2) % 2, pl.ds(pl.multiple_of((step % 2) * 16, 16), 16))
        rows = norm[at].astype(F32)
        inverse = lax.rsqrt(jnp.mean(rows * rows, axis=-1, keepdims=True) + 1e-05)
        norm[at] = (rows * inverse * gain).astype(BF16)
        return 0

    lax.fori_loop(0, 32, normalize, 0)
    norm_across = send(piece(norm, 0, quarter_across), piece(norm, 1, quarter_across), across)

    def forward(slot, blocks, m):
        width = blocks * PAD
        acc[...] = jnp.zeros_like(acc)

        def add(step, _):
            at = columns(step)
            for kind, rows in enumerate((norm, cot)):
                left = rows[m, :, :, :, :, at].reshape(TOK, STEP)
                right = weights[kind, slot : slot + blocks, :, at].reshape(width, STEP)
                acc[kind, :, 0:width] += dot(left, right, (1, 1))
            return 0

        lax.fori_loop(0, D // STEP, add, 0)

        def finish(step, _):
            rows = columns(step, 128)
            hidden, back = acc[0, rows, 0:width], acc[1, rows, 0:width]
            sig = 1.0 / (1.0 + jnp.exp(-hidden))
            active = hidden * sig
            hidden_grad = back * sig * (1.0 + hidden * (1.0 - sig))
            to = pl.ds(pl.multiple_of(m * TOK + step * 128, 128), 128)
            act[to, slot * PAD : slot * PAD + width] = active.astype(BF16)
            act_t[slot * PAD : slot * PAD + width, to] = active.T.astype(BF16)
            hidden_t[slot * PAD : slot * PAD + width, to] = hidden_grad.T.astype(BF16)
            return 0

        lax.fori_loop(0, TOK // 128, finish, 0)

    def backward(slot, blocks, first, last):
        rows = pl.ds(slot * PAD, blocks * PAD)

        def tile(step, _):
            at = columns(step)
            up_part = dot(hidden_t[rows, :], norm[:, :, :, :, :, at].reshape(2 * TOK, STEP), (1, 0))
            terms = weights[0, slot : slot + blocks, :, at].reshape(blocks * PAD, STEP).astype(F32) * up_part
            gain_acc[:, at] += jnp.sum(terms.reshape(blocks * PAD // 8, 8, STEP), axis=0)
            down_part = dot(act_t[rows, :], cot[:, :, :, :, :, at].reshape(2 * TOK, STEP), (1, 0))
            for b in range(blocks):
                grads[0, slot + b, :, at] = up_part[b * PAD : b * PAD + SENT].astype(BF16)
                grads[1, slot + b, :, at] = down_part[b * PAD : b * PAD + SENT].astype(BF16)
            return 0

        lax.fori_loop(first // STEP, last // STEP, tile, 0)

    gain_acc[...] = jnp.zeros_like(gain_acc)
    forward(0, 1, 0)

    onward = []
    for ref, copy in ((cot, cot_across), (norm, norm_across)):
        copy.wait_recv()
        src = piece(ref, 1, quarter)
        onward.append([send(src, src, device) for device in (beside, y_at(1), y_at(3))] + [send(src, src, sibling)])
    up_right.wait_recv()
    up_relay = send(block(0, 2), block(0, 3), z_at(1))
    down_left.wait_recv()
    down_relay = send(block(1, 1), block(1, 3), z_at(3))
    shared = []
    for ref, copies in ((cot, onward[0]), (norm, onward[1])):
        for shift, copy in ((2, copies[0]), (3, copies[1]), (1, copies[2])):
            copy.wait_recv()
            src = piece(ref, 1, (quarter + shift) % 4)
            shared.append(send(src, src, sibling))
    for copy in [onward[0][3], onward[1][3]] + shared:
        copy.wait_recv()

    forward(0, 1, 1)
    down_right.wait_recv()
    up_left.wait_recv()

    def forward_pair(m, _):
        forward(1, 2, m)
        return 0

    lax.fori_loop(0, 2, forward_pair, 0)

    direct = []
    for first, last in HALVES:
        backward(0, 3, first, last)
        at = pl.ds(first, HALF)
        direct.append(
            (
                send(grads.at[1, 1, :, at], mail.at[1, 0, :, at], z_at(1)),
                send(grads.at[0, 2, :, at], mail.at[0, 0, :, at], z_at(3)),
            )
        )

    up_relay.wait_recv()
    down_relay.wait_recv()

    def forward_far(m, _):
        forward(3, 1, m)
        return 0

    lax.fori_loop(0, 2, forward_far, 0)
    far = []
    for first, last in HALVES:
        backward(3, 1, first, last)
        at = pl.ds(first, HALF)
        far.append(
            (
                send(grads.at[0, 3, :, at], mail.at[0, 1, :, at], z_at(1)),
                send(grads.at[1, 3, :, at], mail.at[1, 1, :, at], z_at(3)),
            )
        )

    for copy in [cot_across, norm_across] + onward[0] + onward[1] + shared:
        copy.wait_send()
    pl.semaphore_signal(free_sem, inc=1, device_id=sibling, device_id_type=MESH)
    gain_own[...] = jnp.sum(gain_acc[...], axis=0, keepdims=True)
    gain_core = send(gain_own, gain_slots.at[0, 0], sibling)

    def project(first, last):
        def tile(step, _):
            at = columns(step)
            right = weights[1, :, :, at].reshape(4 * PAD, STEP)
            for m in range(2):
                part = dot(act[m * TOK : (m + 1) * TOK, :], right, (1, 0))
                norm[m, :, :, :, :, at] = part.astype(BF16).reshape(4, 2, 2, 32, STEP)
            return 0

        lax.fori_loop(first // STEP, last // STEP, tile, 0)

    halves = []
    for first, last in HALVES:
        project(first, last)
        if first == 0:
            pl.semaphore_wait(free_sem, 1)
        at = pl.ds(first, HALF)
        halves.append(send(norm.at[:, :, :, 1 - core, :, at], cot.at[:, :, :, 0, :, at], sibling))

    def add_core(first):
        def tile(step, _):
            at = (step // 8, (step // 2) % 4, step % 2)
            cols = pl.ds(first, HALF)
            mine = norm[(*at, core, slice(None), cols)].astype(F32)
            theirs = cot[(*at, 0, slice(None), cols)].astype(F32)
            cot[(*at, 0, slice(None), cols)] = (mine + theirs).astype(BF16)
            return 0

        lax.fori_loop(0, 16, tile, 0)

    def microbatch(cx):
        return (cx // 2 + x_hi) % 2

    left, right = pl.ds(0, HALF), pl.ds(HALF, HALF)
    halves[0].wait_recv()
    add_core(0)
    along_x = []
    for j in range(1, 4):
        to = (x + j) % 4
        along_x.append(send(cot.at[microbatch(to), :, to % 2, 0, :, left], x_first.at[j - 1], x_at(j)))
    halves[1].wait_recv()
    add_core(HALF)
    along_y = []
    for j in range(1, 4):
        along_y.append(send(cot.at[:, (y + j) % 4, :, 0, :, right], y_first.at[j - 1], y_at(j)))

    def spread(stage, place, others):
        gain_slots[stage, place] = gain_own[...]
        return [send(gain_own, gain_slots.at[stage, place], other) for other in others]

    def gather(stage, copies):
        for copy in copies:
            copy.wait()
        gain_own[...] = (gain_slots[stage, 0] + gain_slots[stage, 1]) + (gain_slots[stage, 2] + gain_slots[stage, 3])

    gain_core.wait()
    gain_own[...] = gain_own[...] + gain_slots[0, 0]
    gain_x = spread(1, x, [x_at(j) for j in range(1, 4)])

    last_leg = []
    for half, (first, last) in enumerate(HALVES):
        at = pl.ds(first, HALF)
        for copy in far[half]:
            copy.wait_recv()

        def combine(step, _):
            cols = columns(step)
            grads[0, 1, :, cols] = (grads[0, 1, :, cols].astype(F32) + mail[0, 1, :, cols].astype(F32)).astype(BF16)
            grads[1, 2, :, cols] = (grads[1, 2, :, cols].astype(F32) + mail[1, 1, :, cols].astype(F32)).astype(BF16)
            return 0

        lax.fori_loop(first // STEP, last // STEP, combine, 0)
        last_leg.append(
            (
                send(grads.at[0, 1, :, at], mail.at[0, 2, :, at], z_at(1)),
                send(grads.at[1, 2, :, at], mail.at[1, 2, :, at], z_at(3)),
            )
        )
        if half == 0:
            gather(1, gain_x)
            gain_y = spread(2, y, [y_at(j) for j in range(1, 4)])

    gather(2, gain_y)
    gain_z = spread(3, z, [z_at(j) for j in range(1, 4)])

    for copy in along_x:
        copy.wait()

    def add_x(step, _):
        total = cot[0, step, x_lo, 0, :, left].astype(F32)
        for j in range(3):
            total += x_first[j, step].astype(F32)
        x_first[0, step] = total.astype(BF16)
        return 0

    lax.fori_loop(0, 4, add_x, 0)
    then_y = [send(x_first.at[0, (y + j) % 4], y_second.at[j - 1], y_at(j)) for j in range(1, 4)]
    for copy in along_y:
        copy.wait()

    def add_y(step, _):
        at = (step // 2, step % 2)
        total = cot[(at[0], y, at[1], 0, slice(None), right)].astype(F32)
        for j in range(3):
            total += y_first[(j, *at)].astype(F32)
        y_first[(0, *at)] = total.astype(BF16)
        return 0

    lax.fori_loop(0, 4, add_y, 0)
    then_x = []
    for j in range(1, 4):
        to = (x + j) % 4
        then_x.append(send(y_first.at[0, microbatch(to), to % 2], x_second.at[j - 1], x_at(j)))

    load_own.wait()
    gather(3, gain_z)
    gain_out_ref[...] = gain_own[...] / gain
    for copy in then_y:
        copy.wait()
    total = own_rows[:, left].astype(F32) + x_first[0, y].astype(F32)
    for j in range(3):
        total += y_second[j].astype(F32)
    out_ref[:, left] = total.astype(BF16)
    for copy in then_x:
        copy.wait()
    total = own_rows[:, right].astype(F32) + y_first[0, 0, x_lo].astype(F32)
    for j in range(3):
        total += x_second[j].astype(F32)
    out_ref[:, right] = total.astype(BF16)

    for half, (first, last) in enumerate(HALVES):
        for copy in (*direct[half], *last_leg[half]):
            copy.wait_recv()

        def finish(step, _):
            cols = columns(step)
            for kind, ref in enumerate((grad_up_ref, grad_down_ref)):
                total = grads[kind, 0, :, cols].astype(F32)
                total += mail[kind, 0, :, cols].astype(F32)
                total += mail[kind, 2, :, cols].astype(F32)
                ref[:, cols] = total[0:OWN].astype(BF16)
            return 0

        lax.fori_loop(first // STEP, last // STEP, finish, 0)

    for copy in [up_right, down_left, down_right, up_left, up_relay, down_relay, *halves]:
        copy.wait_send()
    for pairs in (direct, far, last_leg):
        for pair in pairs:
            for copy in pair:
                copy.wait_send()


COPIES = 64


def body(tokens, cotangent, gain, up_weight, down_weight):
    vmem, anywhere = pl.BlockSpec(memory_space=pltpu.VMEM), pl.BlockSpec(memory_space=pl.ANY)
    rows = (1, 4, 2, 2, 32, D)
    out, gain_out, grad_up, grad_down = pl.pallas_call(
        kernel,
        out_shape=(
            jax.ShapeDtypeStruct((32, D), BF16),
            jax.ShapeDtypeStruct((1, D), F32),
            jax.ShapeDtypeStruct((OWN, D), BF16),
            jax.ShapeDtypeStruct((OWN, D), BF16),
        ),
        in_specs=[anywhere, anywhere, vmem, vmem, vmem],
        out_specs=(vmem, vmem, vmem, vmem),
        scratch_shapes=[
            pltpu.VMEM((2, 4, 2, 2, 32, D), BF16),
            pltpu.VMEM((2, 4, 2, 2, 32, D), BF16),
            pltpu.VMEM((2, 4, PAD, D), BF16),
            pltpu.VMEM((2 * TOK, 4 * PAD), BF16),
            pltpu.VMEM((4 * PAD, 2 * TOK), BF16),
            pltpu.VMEM((4 * PAD, 2 * TOK), BF16),
            pltpu.VMEM((2, TOK, 2 * PAD), F32),
            pltpu.VMEM((2, 4, SENT, D), BF16),
            pltpu.VMEM((2, 3, SENT, D), BF16),
            pltpu.VMEM((3, 4, 32, HALF), BF16),
            pltpu.VMEM((3, 2, 2, 32, HALF), BF16),
            pltpu.VMEM((3, 32, HALF), BF16),
            pltpu.VMEM((3, 32, HALF), BF16),
            pltpu.VMEM((32, D), BF16),
            pltpu.VMEM((8, D), F32),
            pltpu.VMEM((1, D), F32),
            pltpu.VMEM((4, 4, 1, D), F32),
            pltpu.SemaphoreType.DMA((COPIES,)),
            pltpu.SemaphoreType.DMA((COPIES,)),
            pltpu.SemaphoreType.DMA((3,)),
            pltpu.SemaphoreType.REGULAR,
        ],
        compiler_params=pltpu.CompilerParams(collective_id=0, has_side_effects=True, vmem_limit_bytes=63 * 2**20),
    )(tokens.reshape(rows), cotangent.reshape(rows), gain[None], up_weight, down_weight)
    return (out[None], gain_out[0], grad_up, grad_down)


def solution(mesh):
    placed = (
        P("blk", None, None),
        P("blk", None, None),
        P(),
        P(("dp", "blk"), None),
        P(("dp", "blk"), None),
    )
    return jax.shard_map(
        body,
        mesh=mesh,
        in_specs=placed,
        out_specs=(P("blk", "dp", None), P(), P(("dp", "blk"), None), P(("dp", "blk"), None)),
        check_vma=False,
    )
```

time: 1040 us -> 170 us (0.16)
  waiting for transfers between devices: 554 us -> 0 us
  blocking collectives: 366 us -> 0 us
  Pallas kernels: 0 us -> 162 us
  matrix products: 58.1 us -> 0 us
  other arithmetic: 20.6 us -> 0 us
  local copies, waits for them, and re-layouts: 20.9 us -> 6.49 us
  between operations: 14.5 us -> 0.64 us
    psum x1 -> x0, blocking collectives: 366 us -> none  [body(): grad_gain = lax.psum(partial_gain, ('dp', 'blk'))]
    unnamed x5 -> x0, waiting for transfers between devices: 342 us -> none
    all_gather x2 -> x0, waiting for transfers between devices: 211 us -> none  [the longest x1 115 us: body(): lax.all_gather(up_weight, 'blk', axis=0, tiled=True)]
    pallas_call x0 -> x1, Pallas kernels: none -> 162 us  [body(): pl.pallas_call(kernel, out_shape=(jax.ShapeDtypeStruct((32, D), BF16), ja...]
    dot_general x6 -> x0, matrix products: 58.1 us -> none  [the longest x1 11.2 us: body(): jnp.dot(hidden_grad, up_all, preferred_element_type=jnp.float32)]
    unnamed x13 -> x6, local copies, waits for them, and re-layouts: 17.4 us -> 6.49 us
  transfers between devices with their start and end apart: 4 -> 0, of which waited for: 3 -> 0; matrix products, arithmetic and copies ran while one was open for 7% -> 0% of each run, Pallas kernels for 0% -> 0%
where the time goes in v1:
time: 170 us; the launch traced here: 169 us
  Pallas kernels  162 us (95%)
  local copies, waits for them, and re-layouts  6.49 us (4%)
    pallas_call x1, Pallas kernels, body(): pl.pallas_call(kernel, out_shape=(jax.ShapeDtypeStruct((32, D), BF16), ja...  162 us
    unnamed x6, local copies, waits for them, and re-layouts  6.49 us

profile of v1, /device:TPU:0, one launch (start us, length us, event | category | flops | bytes accessed | tf_op | source)
XLA Modules:
  0.0 168.7 jit_solution(8848569737951321737)
XLA Ops:
  0.6 161.5 %shard_map.84 = (bf16[32,5120]{1,0:T(8,128)(2,1)}, f32[1,5120]{1,0:T(1,128)}, bf16[108,5120]{1,0:T(8,128)(2,1)}, bf16[108,5120]{1,0:T(8,128)(2,1)}) custom-call(bf16[1,4,2,2,32,5120]{5,4,3,2,1,0:T(8,128)(2,1)} %bitcast.5, bf16[1,4,2,2,32,5120]{5,4,3,2,1,0:T(8,128)(2,1)} %bitcast.6, f32[1,5120]{1,0:T(1,128)} %bitcast.8, bf16[108,5120]{1,0:T(8,128)(2,1)} %up_ref.1, ...), custom_call_target="tpu_custom_call" | custom-call | tf_op jit(solution)/shard_map/pallas_call | solution.py:386
  162.2 1.7 %copy.13 = bf16[1,32,5120]{2,1,0:T(8,128)(2,1)} copy(bf16[1,32,5120]{2,1,0:T(8,128)(2,1)} %bitcast.7) | data formatting | bytes 655360
  163.9 1.3 copy.14
  165.2 0.0 copy-start
  165.2 2.4 %copy.15 = bf16[108,5120]{1,0:T(8,128)(2,1)} copy(bf16[108,5120]{1,0:T(8,128)(2,1)} %get-tuple-element.18) | data formatting | bytes 2211840
  167.7 0.0 copy-done
  167.7 1.0 copy.16
Async XLA Ops:
  165.2 2.4 %copy-start = (bf16[108,5120]{1,0:T(8,128)(2,1)S(1)}, bf16[108,5120]{1,0:T(8,128)(2,1)}, u32[]{:S(2)}) copy-start(bf16[108,5120]{1,0:T(8,128)(2,1)} %get-tuple-element.19) | copy-start | bytes 3317764

commit v2 on v1

v2 whole, which is shorter than its diff:
```python
import jax
import jax.numpy as jnp
from jax import lax
from jax.experimental import pallas as pl
from jax.experimental.pallas import tpu as pltpu
from jax.sharding import PartitionSpec as P

D = 5120
TOK = 512
OWN = 108
MAIN = 96
PAD = 128
STEP = 256
HALF = D // 2
FOURTH = D // 4
TAIL = 3 * FOURTH
MESH = pl.DeviceIdType.MESH
BF16 = jnp.bfloat16
F32 = jnp.float32


def columns(step, size=STEP, first=0):
    return pl.ds(pl.multiple_of(first + step * size, size), size)


def row_numbers(like):
    return lax.broadcasted_iota(jnp.int32, like.shape, 0)


def pack(fourth, last, at):
    return jnp.where(row_numbers(fourth) < 12, fourth, pltpu.roll(last, 12 - 4 * at, 0))


def unpack(fourths):
    row = row_numbers(fourths[0])
    moved = [pltpu.roll(fourth, 4 * at + 4, 0) for at, fourth in enumerate(fourths)]
    last = jnp.where(row < 4, moved[0], jnp.where(row < 8, moved[1], jnp.where(row < 12, moved[2], 0.0)))
    return [jnp.where(row < 12, fourth, 0.0) for fourth in fourths] + [last]


def dot(a, b, over):
    return lax.dot_general(a, b, ((over[:1], over[1:]), ((), ())), preferred_element_type=F32)


def kernel(
    tokens_ref, cotangent_ref, gain_ref, up_ref, down_ref,
    out_ref, gain_out_ref, grad_up_ref, grad_down_ref,
    norm, cot, weights, tails, act, act_t, hidden_t, acc, grads, grad_tails, mail, mail_tails,
    x_first, y_first, y_second, x_second,
    own_rows, gain_acc, gain_own, gain_slots, send_sem, recv_sem, local_sem, free_sem,
):
    dp, blk = lax.axis_index("dp"), lax.axis_index("blk")
    y, x_lo, core = dp // 4, (dp // 2) % 2, dp % 2
    z, x_hi = blk // 2, blk % 2
    x = 2 * x_hi + x_lo

    def chip(cx, cy, cz, cc):
        return (cy * 4 + (cx % 2) * 2 + cc, cz * 2 + cx // 2)

    def x_at(j):
        return chip((x + j) % 4, y, z, core)

    def y_at(j):
        return chip(x, (y + j) % 4, z, core)

    def z_at(j):
        return chip(x, y, (z + j) % 4, core)

    sibling = chip(x, y, z, 1 - core)
    across = chip(3 - x, y, z, core)
    beside = chip(x + 1 - 2 * x_lo, y, z, core)

    count = [0]

    def send(src, dst, device):
        at = count[0]
        count[0] += 1
        copy = pltpu.make_async_remote_copy(
            src_ref=src, dst_ref=dst, send_sem=send_sem.at[at], recv_sem=recv_sem.at[at], device_id=device, device_id_type=MESH
        )
        copy.start()
        return copy

    load_tokens = pltpu.make_async_copy(tokens_ref.at[0], norm.at[0], local_sem.at[0])
    load_cot = pltpu.make_async_copy(cotangent_ref.at[0], cot.at[0], local_sem.at[1])
    load_own = pltpu.make_async_copy(tokens_ref.at[0, y, x_lo, core], own_rows, local_sem.at[2])
    load_tokens.start()
    load_cot.start()
    load_own.start()

    partners = [x_at(1), x_at(2), x_at(3), y_at(1), y_at(2), y_at(3), z_at(1), z_at(2), z_at(3), sibling]
    barrier = pltpu.get_barrier_semaphore()
    for partner in partners:
        pl.semaphore_signal(barrier, inc=1, device_id=partner, device_id_type=MESH)

    def fourth_of(at):
        return pl.ds(at * FOURTH, FOURTH)

    for kind, ref in enumerate((up_ref, down_ref)):
        weights[kind, 0, MAIN:PAD, :] = jnp.zeros((PAD - MAIN, D), BF16)
        weights[kind, 0, 0:OWN, :] = ref[...]
        last = weights[kind, 0, MAIN : MAIN + 16, fourth_of(3)].astype(F32)
        for at in range(3):
            rows = weights[kind, 0, MAIN : MAIN + 16, fourth_of(at)].astype(F32)
            tails[kind, 0, :, fourth_of(at)] = pack(rows, last, at).astype(BF16)
        for slot in range(1, 4):
            weights[kind, slot, MAIN + 16 : PAD, :] = jnp.zeros((PAD - MAIN - 16, D), BF16)
    pl.semaphore_wait(barrier, len(partners))

    def send_block(kind, slot, to, device):
        return [
            send(weights.at[kind, slot, pl.ds(0, MAIN)], weights.at[kind, to, pl.ds(0, MAIN)], device),
            send(tails.at[kind, slot], tails.at[kind, to], device),
        ]

    def wait_recv(copies):
        for copy in copies:
            copy.wait_recv()

    def unpack_block(kind, slot):
        fourths = unpack([tails[kind, slot, :, fourth_of(at)].astype(F32) for at in range(3)])
        for at in range(4):
            weights[kind, slot, MAIN : MAIN + 16, fourth_of(at)] = fourths[at].astype(BF16)

    up_right = send_block(0, 0, 2, z_at(1))
    down_left = send_block(1, 0, 1, z_at(3))
    down_right = send_block(1, 0, 2, z_at(1))
    up_left = send_block(0, 0, 1, z_at(3))

    quarter = (y + 2 * x_lo) % 4
    quarter_across = (y + 2 - 2 * x_lo) % 4

    def piece(ref, which, q):
        return ref.at[which, q, :, core]

    load_cot.wait()
    cot_across = send(piece(cot, 0, quarter_across), piece(cot, 1, quarter_across), across)

    load_tokens.wait()
    gain = gain_ref[...]

    def normalize(step, _):
        at = (0, step // 8, (step // 4) % 2, (step // 2) % 2, pl.ds(pl.multiple_of((step % 2) * 16, 16), 16))
        rows = norm[at].astype(F32)
        inverse = lax.rsqrt(jnp.mean(rows * rows, axis=-1, keepdims=True) + 1e-05)
        norm[at] = (rows * inverse * gain).astype(BF16)
        return 0

    lax.fori_loop(0, 32, normalize, 0)
    norm_across = send(piece(norm, 0, quarter_across), piece(norm, 1, quarter_across), across)

    def forward(slot, blocks, micros):
        width = blocks * PAD
        tall = len(micros) * TOK
        first_row = micros[0] * TOK
        which = slice(micros[0], micros[0] + len(micros))

        for kind, rows in enumerate((norm, cot)):
            left = rows[which].reshape(tall, D)
            right = weights[kind, slot : slot + blocks].reshape(width, D)
            acc[kind, 0:tall, 0:width] = dot(left, right, (1, 1))

        def finish(step, _):
            rows = columns(step, 128)
            hidden, back = acc[0, rows, 0:width], acc[1, rows, 0:width]
            sig = 1.0 / (1.0 + jnp.exp(-hidden))
            active = hidden * sig
            hidden_grad = back * sig * (1.0 + hidden * (1.0 - sig))
            to = columns(step, 128, first_row)
            act[to, slot * PAD : slot * PAD + width] = active.astype(BF16)
            act_t[slot * PAD : slot * PAD + width, to] = active.T.astype(BF16)
            hidden_t[slot * PAD : slot * PAD + width, to] = hidden_grad.T.astype(BF16)
            return 0

        lax.fori_loop(0, tall // 128, finish, 0)

    def backward(slot, blocks, fourth):
        rows = pl.ds(slot * PAD, blocks * PAD)

        at = fourth_of(fourth)
        up_part = dot(hidden_t[rows, :], norm[:, :, :, :, :, at].reshape(2 * TOK, FOURTH), (1, 0))
        terms = weights[0, slot : slot + blocks, :, at].reshape(blocks * PAD, FOURTH).astype(F32) * up_part
        gain_acc[:, at] += jnp.sum(terms.reshape(blocks * PAD // 8, 8, FOURTH), axis=0)
        down_part = dot(act_t[rows, :], cot[:, :, :, :, :, at].reshape(2 * TOK, FOURTH), (1, 0))
        for kind, part in enumerate((up_part, down_part)):
            for b in range(blocks):
                grads[kind, slot + b, :, at] = part[b * PAD : b * PAD + MAIN].astype(BF16)
                end = part[b * PAD + MAIN : b * PAD + MAIN + 16]
                if fourth < 3:
                    grad_tails[kind, slot + b, :, at] = end.astype(BF16)
                    continue
                for other in range(3):
                    to = fourth_of(other)
                    mixed = pack(grad_tails[kind, slot + b, :, to].astype(F32), end, other)
                    grad_tails[kind, slot + b, :, to] = mixed.astype(BF16)

    def send_grads(part, kind, slot, to, device):
        if part == 2:
            return send(grad_tails.at[kind, slot], mail_tails.at[kind, to], device)
        at = pl.ds(part * HALF, HALF)
        return send(grads.at[kind, slot, :, at], mail.at[kind, to, :, at], device)

    gain_acc[...] = jnp.zeros_like(gain_acc)
    forward(0, 1, (0,))

    onward = []
    for ref, copy in ((cot, cot_across), (norm, norm_across)):
        copy.wait_recv()
        src = piece(ref, 1, quarter)
        onward.append([send(src, src, device) for device in (beside, y_at(1), y_at(3))] + [send(src, src, sibling)])
    wait_recv(up_right)
    up_relay = send_block(0, 2, 3, z_at(1))
    wait_recv(down_left)
    down_relay = send_block(1, 1, 3, z_at(3))
    shared = []
    for ref, copies in ((cot, onward[0]), (norm, onward[1])):
        for shift, copy in ((2, copies[0]), (3, copies[1]), (1, copies[2])):
            copy.wait_recv()
            src = piece(ref, 1, (quarter + shift) % 4)
            shared.append(send(src, src, sibling))
    for copy in [onward[0][3], onward[1][3]] + shared:
        copy.wait_recv()

    forward(0, 1, (1,))
    wait_recv(down_right)
    wait_recv(up_left)
    for kind in range(2):
        unpack_block(kind, 1)
        unpack_block(kind, 2)
    forward(1, 2, (0, 1))

    direct = []
    for fourth in range(4):
        backward(0, 3, fourth)
        for part in ((), (0,), (), (1, 2))[fourth]:
            direct.append((send_grads(part, 1, 1, 0, z_at(1)), send_grads(part, 0, 2, 0, z_at(3))))

    wait_recv(up_relay)
    wait_recv(down_relay)
    for kind in range(2):
        unpack_block(kind, 3)
    forward(3, 1, (0, 1))

    for copy in [cot_across, norm_across] + onward[0] + onward[1] + shared:
        copy.wait_send()

    def project(fourth):
        def tile(step, _):
            at = columns(step, STEP, fourth * FOURTH)
            right = weights[1, :, :, at].reshape(4 * PAD, STEP)
            for m in range(2):
                part = dot(act[m * TOK : (m + 1) * TOK, :], right, (1, 0))
                norm[m, :, :, :, :, at] = part.astype(BF16).reshape(4, 2, 2, 32, STEP)
            return 0

        lax.fori_loop(0, FOURTH // STEP, tile, 0)

    def add_core(fourth):
        cols = fourth_of(fourth)

        def tile(step, _):
            at = (step // 8, (step // 2) % 4, step % 2)
            mine = norm[(*at, core, slice(None), cols)].astype(F32)
            theirs = cot[(*at, 0, slice(None), cols)].astype(F32)
            cot[(*at, 0, slice(None), cols)] = (mine + theirs).astype(BF16)
            return 0

        lax.fori_loop(0, 16, tile, 0)

    def microbatch(cx):
        return (cx // 2 + x_hi) % 2

    def first_leg(fourth):
        cores[fourth].wait_recv()
        add_core(fourth)
        cols, turn = fourth_of(fourth), fourth // 2
        copies = []
        for j in range(1, 4):
            to = (x + j) % 4
            if fourth % 2 == 0:
                copies.append(send(cot.at[microbatch(to), :, to % 2, 0, :, cols], x_first.at[turn, j - 1], x_at(j)))
            else:
                copies.append(send(cot.at[:, (y + j) % 4, :, 0, :, cols], y_first.at[turn, j - 1], y_at(j)))
        legs.append(copies)

    def second_leg(fourth):
        for copy in legs[fourth]:
            copy.wait()
        cols, turn = fourth_of(fourth), fourth // 2

        def add(step, _):
            if fourth % 2 == 0:
                total = cot[0, step, x_lo, 0, :, cols].astype(F32)
                for j in range(3):
                    total += x_first[turn, j, step].astype(F32)
                x_first[turn, 0, step] = total.astype(BF16)
            else:
                at = (step // 2, step % 2)
                total = cot[(at[0], y, at[1], 0, slice(None), cols)].astype(F32)
                for j in range(3):
                    total += y_first[(turn, j, *at)].astype(F32)
                y_first[(turn, 0, *at)] = total.astype(BF16)
            return 0

        lax.fori_loop(0, 4, add, 0)
        copies = []
        for j in range(1, 4):
            to = (x + j) % 4
            if fourth % 2 == 0:
                copies.append(send(x_first.at[turn, 0, (y + j) % 4], y_second.at[turn, j - 1], y_at(j)))
            else:
                copies.append(send(y_first.at[turn, 0, microbatch(to), to % 2], x_second.at[turn, j - 1], x_at(j)))
        legs[fourth] = copies

    def last_sum(fourth):
        for copy in legs[fourth]:
            copy.wait()
        cols, turn = fourth_of(fourth), fourth // 2
        if fourth % 2 == 0:
            total, others = x_first[turn, 0, y], y_second
        else:
            total, others = y_first[turn, 0, 0, x_lo], x_second
        total = own_rows[:, cols].astype(F32) + total.astype(F32)
        for j in range(3):
            total += others[turn, j].astype(F32)
        out_ref[:, cols] = total.astype(BF16)

    far, cores, legs = [], [], []
    for fourth in range(4):
        backward(3, 1, fourth)
        for part in ((), (0,), (), (1, 2))[fourth]:
            far.append((send_grads(part, 0, 3, 1, z_at(1)), send_grads(part, 1, 3, 1, z_at(3))))
        pl.semaphore_signal(free_sem, inc=1, device_id=sibling, device_id_type=MESH)
        project(fourth)
        pl.semaphore_wait(free_sem, 1)
        cols = fourth_of(fourth)
        cores.append(send(norm.at[:, :, :, 1 - core, :, cols], cot.at[:, :, :, 0, :, cols], sibling))
        if fourth > 0:
            first_leg(fourth - 1)
    gain_own[...] = jnp.sum(gain_acc[...], axis=0, keepdims=True)
    gain_core = send(gain_own, gain_slots.at[0, 0], sibling)
    first_leg(3)

    def spread(stage, place, others):
        gain_slots[stage, place] = gain_own[...]
        return [send(gain_own, gain_slots.at[stage, place], other) for other in others]

    def gather(stage, copies):
        for copy in copies:
            copy.wait()
        gain_own[...] = (gain_slots[stage, 0] + gain_slots[stage, 1]) + (gain_slots[stage, 2] + gain_slots[stage, 3])

    gain_core.wait()
    gain_own[...] = gain_own[...] + gain_slots[0, 0]
    gain_x = spread(1, x, [x_at(j) for j in range(1, 4)])

    last_leg = []

    def combine(part):
        for copy in far[part]:
            copy.wait_recv()
        pairs = ((0, 1), (1, 2))
        if part == 2:
            for kind, slot in pairs:
                total = grad_tails[kind, slot].astype(F32) + mail_tails[kind, 1].astype(F32)
                grad_tails[kind, slot] = total.astype(BF16)
        else:

            def tile(step, _):
                cols = columns(step, 512, part * HALF)
                for kind, slot in pairs:
                    total = grads[kind, slot, :, cols].astype(F32) + mail[kind, 1, :, cols].astype(F32)
                    grads[kind, slot, :, cols] = total.astype(BF16)
                return 0

            lax.fori_loop(0, HALF // 512, tile, 0)
        last_leg.append((send_grads(part, 0, 1, 2, z_at(1)), send_grads(part, 1, 2, 2, z_at(3))))

    gather(1, gain_x)
    gain_y = spread(2, y, [y_at(j) for j in range(1, 4)])
    second_leg(0)
    second_leg(1)
    combine(0)
    gather(2, gain_y)
    gain_z = spread(3, z, [z_at(j) for j in range(1, 4)])
    second_leg(2)
    second_leg(3)
    combine(1)
    combine(2)

    gather(3, gain_z)
    gain_out_ref[...] = gain_own[...] / gain
    load_own.wait()
    for fourth in range(4):
        last_sum(fourth)

    outputs = (grad_up_ref, grad_down_ref)
    for part in range(3):
        for copy in (*direct[part], *last_leg[part]):
            copy.wait_recv()
        if part == 2:
            for kind, ref in enumerate(outputs):
                fourths = []
                for at in range(3):
                    cols = fourth_of(at)
                    total = grad_tails[kind, 0, :, cols].astype(F32)
                    total += mail_tails[kind, 0, :, cols].astype(F32)
                    total += mail_tails[kind, 2, :, cols].astype(F32)
                    fourths.append(total)
                for at, rows in enumerate(unpack(fourths)):
                    ref[MAIN:OWN, fourth_of(at)] = rows[0 : OWN - MAIN].astype(BF16)
            continue

        def finish(step, _):
            cols = columns(step, 512, part * HALF)
            for kind, ref in enumerate(outputs):
                total = grads[kind, 0, :, cols].astype(F32)
                total += mail[kind, 0, :, cols].astype(F32)
                total += mail[kind, 2, :, cols].astype(F32)
                ref[0:MAIN, cols] = total.astype(BF16)
            return 0

        lax.fori_loop(0, HALF // 512, finish, 0)

    for copies in (up_right, down_left, down_right, up_left, up_relay, down_relay, cores, *direct, *far, *last_leg):
        for copy in copies:
            copy.wait_send()


def copy_kernel(*refs):
    for src, dst in zip(refs[:4], refs[4:]):
        dst[...] = src[...]


COPIES = 96


def body(tokens, cotangent, gain, up_weight, down_weight):
    vmem, anywhere = pl.BlockSpec(memory_space=pltpu.VMEM), pl.BlockSpec(memory_space=pl.ANY)
    rows = (1, 4, 2, 2, 32, D)
    results = (
        jax.ShapeDtypeStruct((32, D), BF16),
        jax.ShapeDtypeStruct((1, D), F32),
        jax.ShapeDtypeStruct((OWN, D), BF16),
        jax.ShapeDtypeStruct((OWN, D), BF16),
    )
    parts = pl.pallas_call(
        kernel,
        out_shape=results,
        in_specs=[anywhere, anywhere, vmem, vmem, vmem],
        out_specs=(vmem, vmem, vmem, vmem),
        scratch_shapes=[
            pltpu.VMEM((2, 4, 2, 2, 32, D), BF16),
            pltpu.VMEM((2, 4, 2, 2, 32, D), BF16),
            pltpu.VMEM((2, 4, PAD, D), BF16),
            pltpu.VMEM((2, 4, 16, TAIL), BF16),
            pltpu.VMEM((2 * TOK, 4 * PAD), BF16),
            pltpu.VMEM((4 * PAD, 2 * TOK), BF16),
            pltpu.VMEM((4 * PAD, 2 * TOK), BF16),
            pltpu.VMEM((2, 2 * TOK, 2 * PAD), F32),
            pltpu.VMEM((2, 4, MAIN, D), BF16),
            pltpu.VMEM((2, 4, 16, TAIL), BF16),
            pltpu.VMEM((2, 3, MAIN, D), BF16),
            pltpu.VMEM((2, 3, 16, TAIL), BF16),
            pltpu.VMEM((2, 3, 4, 32, FOURTH), BF16),
            pltpu.VMEM((2, 3, 2, 2, 32, FOURTH), BF16),
            pltpu.VMEM((2, 3, 32, FOURTH), BF16),
            pltpu.VMEM((2, 3, 32, FOURTH), BF16),
            pltpu.VMEM((32, D), BF16),
            pltpu.VMEM((8, D), F32),
            pltpu.VMEM((1, D), F32),
            pltpu.VMEM((4, 4, 1, D), F32),
            pltpu.SemaphoreType.DMA((COPIES,)),
            pltpu.SemaphoreType.DMA((COPIES,)),
            pltpu.SemaphoreType.DMA((3,)),
            pltpu.SemaphoreType.REGULAR,
        ],
        compiler_params=pltpu.CompilerParams(collective_id=0, has_side_effects=True, vmem_limit_bytes=63 * 2**20),
    )(tokens.reshape(rows), cotangent.reshape(rows), gain[None], up_weight, down_weight)
    out, gain_out, grad_up, grad_down = pl.pallas_call(
        copy_kernel,
        out_shape=results,
        in_specs=[vmem] * 4,
        out_specs=(vmem,) * 4,
    )(*parts)
    return (out[None], gain_out[0], grad_up, grad_down)


def solution(mesh):
    placed = (
        P("blk", None, None),
        P("blk", None, None),
        P(),
        P(("dp", "blk"), None),
        P(("dp", "blk"), None),
    )
    return jax.shard_map(
        body,
        mesh=mesh,
        in_specs=placed,
        out_specs=(P("blk", "dp", None), P(), P(("dp", "blk"), None), P(("dp", "blk"), None)),
        check_vma=False,
    )
```

time: 170 us -> 161 us (0.947)
  local copies, waits for them, and re-layouts: 6.49 us -> 0 us
    unnamed x6 -> x0, local copies, waits for them, and re-layouts: 6.49 us -> none
    pallas_call x1 -> x2, Pallas kernels: 162 us -> 161 us  [the longest x1 157 us: body(): pl.pallas_call(kernel, out_shape=results, in_specs=[anywhere, anywhere, v...]
where the time goes in v2:
time: 161 us
  Pallas kernels  161 us (100%)
    pallas_call x1, Pallas kernels, body(): pl.pallas_call(kernel, out_shape=results, in_specs=[anywhere, anywhere, v...  157 us
    pallas_call x1, Pallas kernels, body(): pl.pallas_call(copy_kernel, out_shape=results, in_specs=[vmem] * 4, out_s...  3.24 us

profile of v2, /device:TPU:0, one launch (start us, length us, event | category | flops | bytes accessed | tf_op | source)
XLA Modules:
  0.0 161.3 jit_solution(786742389041709408)
XLA Ops:
  0.6 157.4 %shard_map.84 = (bf16[32,5120]{1,0:T(8,128)(2,1)}, f32[1,5120]{1,0:T(1,128)}, bf16[108,5120]{1,0:T(8,128)(2,1)}, bf16[108,5120]{1,0:T(8,128)(2,1)}) custom-call(bf16[1,4,2,2,32,5120]{5,4,3,2,1,0:T(8,128)(2,1)} %bitcast.5, bf16[1,4,2,2,32,5120]{5,4,3,2,1,0:T(8,128)(2,1)} %bitcast.6, f32[1,5120]{1,0:T(1,128)} %bitcast.7, bf16[108,5120]{1,0:T(8,128)(2,1)} %up_ref.1, ...), custom_call_target="tpu_custom_call" | custom-call | tf_op jit(solution)/shard_map/pallas_call | solution.py:447
  158.0 3.2 %shard_map.85 = (bf16[32,5120]{1,0:T(8,128)(2,1)}, f32[1,5120]{1,0:T(1,128)}, bf16[108,5120]{1,0:T(8,128)(2,1)}, bf16[108,5120]{1,0:T(8,128)(2,1)}) custom-call(bf16[32,5120]{1,0:T(8,128)(2,1)} %get-tuple-element.12.refs_0_, f32[1,5120]{1,0:T(1,128)} %get-tuple-element.13.refs_1_, bf16[108,5120]{1,0:T(8,128)(2,1)} %get-tuple-element.14.refs_2_, ...), custom_call_target="tpu_custom_call" | custom-call | tf_op jit(solution)/shard_map/pallas_call | solution.py:480

commit v3 on v2

--- a/solution.py
+++ b/solution.py
@@ -45,9 +45,9 @@
 def kernel(
     tokens_ref, cotangent_ref, gain_ref, up_ref, down_ref,
     out_ref, gain_out_ref, grad_up_ref, grad_down_ref,
-    norm, cot, weights, tails, act, act_t, hidden_t, acc, grads, grad_tails, mail, mail_tails,
+    own, norm, cot, weights, tails, act, act_t, hidden_t, acc, grads, grad_tails, mail, mail_tails,
     x_first, y_first, y_second, x_second,
-    own_rows, gain_acc, gain_own, gain_slots, send_sem, recv_sem, local_sem, free_sem,
+    own_rows, gain_acc, gain_own, gain_other, gain_half, gain_halves, gain_slots, send_sem, recv_sem, local_sem, free_sem,
 ):
     dp, blk = lax.axis_index("dp"), lax.axis_index("blk")
     y, x_lo, core = dp // 4, (dp // 2) % 2, dp % 2
@@ -81,6 +81,9 @@
         copy.start()
         return copy
 
+    loads = [pltpu.make_async_copy(ref, own.at[kind], local_sem.at[3 + kind]) for kind, ref in enumerate((up_ref, down_ref))]
+    for load in loads:
+        load.start()
     load_tokens = pltpu.make_async_copy(tokens_ref.at[0], norm.at[0], local_sem.at[0])
     load_cot = pltpu.make_async_copy(cotangent_ref.at[0], cot.at[0], local_sem.at[1])
     load_own = pltpu.make_async_copy(tokens_ref.at[0, y, x_lo, core], own_rows, local_sem.at[2])
@@ -96,16 +99,34 @@
     def fourth_of(at):
         return pl.ds(at * FOURTH, FOURTH)
 
-    for kind, ref in enumerate((up_ref, down_ref)):
+    pl.semaphore_wait(barrier, len(partners))
+    for load in loads:
+        load.wait()
+
+    def send_main(kind, to, device):
+        return send(own.at[kind, pl.ds(0, MAIN)], weights.at[kind, to, pl.ds(0, MAIN)], device)
+
+    def send_tail(kind, to, device):
+        return send(tails.at[kind, 0], tails.at[kind, to], device)
+
+    up_right, down_left = [send_main(0, 2, z_at(1))], [send_main(1, 1, z_at(3))]
+    down_right, up_left = [send_main(1, 2, z_at(1))], [send_main(0, 1, z_at(3))]
+
+    for kind in range(2):
         weights[kind, 0, MAIN:PAD, :] = jnp.zeros((PAD - MAIN, D), BF16)
-        weights[kind, 0, 0:OWN, :] = ref[...]
+        weights[kind, 0, MAIN:OWN, :] = own[kind, MAIN:OWN, :]
         last = weights[kind, 0, MAIN : MAIN + 16, fourth_of(3)].astype(F32)
         for at in range(3):
             rows = weights[kind, 0, MAIN : MAIN + 16, fourth_of(at)].astype(F32)
             tails[kind, 0, :, fourth_of(at)] = pack(rows, last, at).astype(BF16)
+    up_right.append(send_tail(0, 2, z_at(1)))
+    down_left.append(send_tail(1, 1, z_at(3)))
+    down_right.append(send_tail(1, 2, z_at(1)))
+    up_left.append(send_tail(0, 1, z_at(3)))
+    for kind in range(2):
+        weights[kind, 0, 0:MAIN, :] = own[kind, 0:MAIN, :]
         for slot in range(1, 4):
             weights[kind, slot, MAIN + 16 : PAD, :] = jnp.zeros((PAD - MAIN - 16, D), BF16)
-    pl.semaphore_wait(barrier, len(partners))
 
     def send_block(kind, slot, to, device):
         return [
@@ -121,11 +142,6 @@
         fourths = unpack([tails[kind, slot, :, fourth_of(at)].astype(F32) for at in range(3)])
         for at in range(4):
             weights[kind, slot, MAIN : MAIN + 16, fourth_of(at)] = fourths[at].astype(BF16)
-
-    up_right = send_block(0, 0, 2, z_at(1))
-    down_left = send_block(1, 0, 1, z_at(3))
-    down_right = send_block(1, 0, 2, z_at(1))
-    up_left = send_block(0, 0, 1, z_at(3))
 
     quarter = (y + 2 * x_lo) % 4
     quarter_across = (y + 2 - 2 * x_lo) % 4
@@ -230,10 +246,14 @@
     forward(1, 2, (0, 1))
 
     direct = []
+
+    def send_direct(part):
+        direct.append((send_grads(part, 1, 1, 0, z_at(1)), send_grads(part, 0, 2, 0, z_at(3))))
+
     for fourth in range(4):
         backward(0, 3, fourth)
         for part in ((), (0,), (), (1, 2))[fourth]:
-            direct.append((send_grads(part, 1, 1, 0, z_at(1)), send_grads(part, 0, 2, 0, z_at(3))))
+            send_direct(part)
 
     wait_recv(up_relay)
     wait_recv(down_relay)
@@ -326,33 +346,45 @@
         out_ref[:, cols] = total.astype(BF16)
 
     far, cores, legs = [], [], []
-    for fourth in range(4):
-        backward(3, 1, fourth)
-        for part in ((), (0,), (), (1, 2))[fourth]:
-            far.append((send_grads(part, 0, 3, 1, z_at(1)), send_grads(part, 1, 3, 1, z_at(3))))
-        pl.semaphore_signal(free_sem, inc=1, device_id=sibling, device_id_type=MESH)
+
+    def send_far(part):
+        far.append((send_grads(part, 0, 3, 1, z_at(1)), send_grads(part, 1, 3, 1, z_at(3))))
+
+    def share(fourth):
         project(fourth)
         pl.semaphore_wait(free_sem, 1)
         cols = fourth_of(fourth)
         cores.append(send(norm.at[:, :, :, 1 - core, :, cols], cot.at[:, :, :, 0, :, cols], sibling))
-        if fourth > 0:
-            first_leg(fourth - 1)
+
+    for fourth in range(4):
+        backward(3, 1, fourth)
+        pl.semaphore_signal(free_sem, inc=1, device_id=sibling, device_id_type=MESH)
+        if fourth == 1:
+            send_far(0)
+            share(0)
+        if fourth == 3:
+            send_far(1)
+            send_far(2)
+    for fourth in range(1, 4):
+        share(fourth)
+        first_leg(fourth - 1)
     gain_own[...] = jnp.sum(gain_acc[...], axis=0, keepdims=True)
-    gain_core = send(gain_own, gain_slots.at[0, 0], sibling)
+    gain_core = send(gain_own, gain_other, sibling)
     first_leg(3)
 
     def spread(stage, place, others):
-        gain_slots[stage, place] = gain_own[...]
-        return [send(gain_own, gain_slots.at[stage, place], other) for other in others]
+        gain_slots[stage, place] = gain_half[...]
+        return [send(gain_half, gain_slots.at[stage, place], other) for other in others]
 
     def gather(stage, copies):
         for copy in copies:
             copy.wait()
-        gain_own[...] = (gain_slots[stage, 0] + gain_slots[stage, 1]) + (gain_slots[stage, 2] + gain_slots[stage, 3])
+        gain_half[...] = (gain_slots[stage, 0] + gain_slots[stage, 1]) + (gain_slots[stage, 2] + gain_slots[stage, 3])
 
     gain_core.wait()
-    gain_own[...] = gain_own[...] + gain_slots[0, 0]
-    gain_x = spread(1, x, [x_at(j) for j in range(1, 4)])
+    own_half = pl.ds(pl.multiple_of(core * HALF, HALF), HALF)
+    gain_half[...] = gain_own[:, own_half] + gain_other[:, own_half]
+    gain_z = spread(0, z, [z_at(j) for j in range(1, 4)])
 
     last_leg = []
 
@@ -376,29 +408,36 @@
             lax.fori_loop(0, HALF // 512, tile, 0)
         last_leg.append((send_grads(part, 0, 1, 2, z_at(1)), send_grads(part, 1, 2, 2, z_at(3))))
 
-    gather(1, gain_x)
-    gain_y = spread(2, y, [y_at(j) for j in range(1, 4)])
     second_leg(0)
     second_leg(1)
     combine(0)
-    gather(2, gain_y)
-    gain_z = spread(3, z, [z_at(j) for j in range(1, 4)])
     second_leg(2)
-    second_leg(3)
     combine(1)
     combine(2)
-
-    gather(3, gain_z)
-    gain_out_ref[...] = gain_own[...] / gain
+    second_leg(3)
+
     load_own.wait()
-    for fourth in range(4):
-        last_sum(fourth)
+    gather(0, gain_z)
+    gain_x = spread(1, x, [x_at(j) for j in range(1, 4)])
+    last_sum(0)
+    last_sum(1)
+    gather(1, gain_x)
+    gain_y = spread(2, y, [y_at(j) for j in range(1, 4)])
+    last_sum(2)
+    last_sum(3)
+    gather(2, gain_y)
+    gain_last = send(gain_half, gain_halves.at[core], sibling)
+    gain_halves[core] = gain_half[...]
 
     outputs = (grad_up_ref, grad_down_ref)
     for part in range(3):
         for copy in (*direct[part], *last_leg[part]):
             copy.wait_recv()
         if part == 2:
+            gain_last.wait()
+            for at in range(2):
+                cols = pl.ds(at * HALF, HALF)
+                gain_out_ref[:, cols] = gain_halves[at] / gain_ref[:, cols]
             for kind, ref in enumerate(outputs):
                 fourths = []
                 for at in range(3):
@@ -428,8 +467,16 @@
 
 
 def copy_kernel(*refs):
-    for src, dst in zip(refs[:4], refs[4:]):
-        dst[...] = src[...]
+    sources, targets, held, sems = refs[:4], refs[4:8], refs[8:12], refs[12]
+    loads = [pltpu.make_async_copy(sources[i], held[i], sems.at[0, i]) for i in range(4)]
+    stores = [pltpu.make_async_copy(held[i], targets[i], sems.at[1, i]) for i in range(4)]
+    for load in loads:
+        load.start()
+    for load, store in zip(loads, stores):
+        load.wait()
+        store.start()
+    for store in stores:
+        store.wait()
 
 
 COPIES = 96
@@ -447,9 +494,10 @@
     parts = pl.pallas_call(
         kernel,
         out_shape=results,
-        in_specs=[anywhere, anywhere, vmem, vmem, vmem],
+        in_specs=[anywhere, anywhere, vmem, anywhere, anywhere],
         out_specs=(vmem, vmem, vmem, vmem),
         scratch_shapes=[
+            pltpu.VMEM((2, OWN, D), BF16),
             pltpu.VMEM((2, 4, 2, 2, 32, D), BF16),
             pltpu.VMEM((2, 4, 2, 2, 32, D), BF16),
             pltpu.VMEM((2, 4, PAD, D), BF16),
@@ -469,10 +517,13 @@
             pltpu.VMEM((32, D), BF16),
             pltpu.VMEM((8, D), F32),
             pltpu.VMEM((1, D), F32),
-            pltpu.VMEM((4, 4, 1, D), F32),
+            pltpu.VMEM((1, D), F32),
+            pltpu.VMEM((1, HALF), F32),
+            pltpu.VMEM((2, 1, HALF), F32),
+            pltpu.VMEM((3, 4, 1, HALF), F32),
             pltpu.SemaphoreType.DMA((COPIES,)),
             pltpu.SemaphoreType.DMA((COPIES,)),
-            pltpu.SemaphoreType.DMA((3,)),
+            pltpu.SemaphoreType.DMA((5,)),
             pltpu.SemaphoreType.REGULAR,
         ],
         compiler_params=pltpu.CompilerParams(collective_id=0, has_side_effects=True, vmem_limit_bytes=63 * 2**20),
@@ -480,8 +531,9 @@
     out, gain_out, grad_up, grad_down = pl.pallas_call(
         copy_kernel,
         out_shape=results,
-        in_specs=[vmem] * 4,
-        out_specs=(vmem,) * 4,
+        in_specs=[anywhere] * 4,
+        out_specs=(anywhere,) * 4,
+        scratch_shapes=[pltpu.VMEM(part.shape, part.dtype) for part in results] + [pltpu.SemaphoreType.DMA((2, 4))],
     )(*parts)
     return (out[None], gain_out[0], grad_up, grad_down)
 

time: 161 us -> 158 us (0.981)
  Pallas kernels: 161 us -> 157 us
    pallas_call x1, Pallas kernels: 157 us -> 155 us  [body(): pl.pallas_call(kernel, out_shape=results, in_specs=[anywhere, anywhere, v...]
where the time goes in v3:
time: 158 us
  Pallas kernels  157 us (99%)
    pallas_call x1, Pallas kernels, body(): pl.pallas_call(kernel, out_shape=results, in_specs=[anywhere, anywhere, v...  155 us

profile of v3, /device:TPU:0, one launch (start us, length us, event | category | flops | bytes accessed | tf_op | source)
XLA Modules:
  0.0 158.3 jit_solution(518465868841045687)
XLA Ops:
  0.6 154.6 %shard_map.84 = (bf16[32,5120]{1,0:T(8,128)(2,1)}, f32[1,5120]{1,0:T(1,128)}, bf16[108,5120]{1,0:T(8,128)(2,1)}, bf16[108,5120]{1,0:T(8,128)(2,1)}) custom-call(bf16[1,4,2,2,32,5120]{5,4,3,2,1,0:T(8,128)(2,1)} %bitcast.5, bf16[1,4,2,2,32,5120]{5,4,3,2,1,0:T(8,128)(2,1)} %bitcast.6, f32[1,5120]{1,0:T(1,128)} %bitcast.7, bf16[108,5120]{1,0:T(8,128)(2,1)} %up_ref.1, ...), custom_call_target="tpu_custom_call" | custom-call | tf_op jit(solution)/shard_map/pallas_call | solution.py:494
  155.2 2.8 %shard_map.85 = (bf16[32,5120]{1,0:T(8,128)(2,1)}, f32[1,5120]{1,0:T(1,128)}, bf16[108,5120]{1,0:T(8,128)(2,1)}, bf16[108,5120]{1,0:T(8,128)(2,1)}) custom-call(bf16[32,5120]{1,0:T(8,128)(2,1)} %get-tuple-element.12.refs_0_, f32[1,5120]{1,0:T(1,128)} %get-tuple-element.13.refs_1_, bf16[108,5120]{1,0:T(8,128)(2,1)} %get-tuple-element.14.refs_2_, ...), custom_call_target="tpu_custom_call" | custom-call | tf_op jit(solution)/shard_map/pallas_call | solution.py:531

commit v4 on v3

--- a/solution.py
+++ b/solution.py
@@ -44,10 +44,10 @@
 
 def kernel(
     tokens_ref, cotangent_ref, gain_ref, up_ref, down_ref,
-    out_ref, gain_out_ref, grad_up_ref, grad_down_ref,
+    out_ref, gain_out_ref, sum_ref, sum_tail_ref, last_tail_ref,
     own, norm, cot, weights, tails, act, act_t, hidden_t, acc, grads, grad_tails, mail, mail_tails,
     x_first, y_first, y_second, x_second,
-    own_rows, gain_acc, gain_own, gain_other, gain_half, gain_halves, gain_slots, send_sem, recv_sem, local_sem, free_sem,
+    own_rows, out_rows, gain_acc, gain_own, gain_other, gain_half, gain_halves, gain_slots, send_sem, recv_sem, local_sem, store_sem, free_sem,
 ):
     dp, blk = lax.axis_index("dp"), lax.axis_index("blk")
     y, x_lo, core = dp // 4, (dp // 2) % 2, dp % 2
@@ -100,18 +100,18 @@
         return pl.ds(at * FOURTH, FOURTH)
 
     pl.semaphore_wait(barrier, len(partners))
+
+    def send_main(kind, to, device):
+        return send((up_ref, down_ref)[kind].at[pl.ds(0, MAIN)], weights.at[kind, to, pl.ds(0, MAIN)], device)
+
+    def send_tail(kind, to, device):
+        return send(tails.at[kind, 0], tails.at[kind, to], device)
+
+    up_right, down_left = [send_main(0, 2, z_at(1))], [send_main(1, 1, z_at(3))]
+    down_right, up_left = [send_main(1, 2, z_at(1))], [send_main(0, 1, z_at(3))]
+
     for load in loads:
         load.wait()
-
-    def send_main(kind, to, device):
-        return send(own.at[kind, pl.ds(0, MAIN)], weights.at[kind, to, pl.ds(0, MAIN)], device)
-
-    def send_tail(kind, to, device):
-        return send(tails.at[kind, 0], tails.at[kind, to], device)
-
-    up_right, down_left = [send_main(0, 2, z_at(1))], [send_main(1, 1, z_at(3))]
-    down_right, up_left = [send_main(1, 2, z_at(1))], [send_main(0, 1, z_at(3))]
-
     for kind in range(2):
         weights[kind, 0, MAIN:PAD, :] = jnp.zeros((PAD - MAIN, D), BF16)
         weights[kind, 0, MAIN:OWN, :] = own[kind, MAIN:OWN, :]
@@ -212,7 +212,8 @@
 
     def send_grads(part, kind, slot, to, device):
         if part == 2:
-            return send(grad_tails.at[kind, slot], mail_tails.at[kind, to], device)
+            target = last_tail_ref.at[kind] if to == 2 else mail_tails.at[kind, to]
+            return send(grad_tails.at[kind, slot], target, device)
         at = pl.ds(part * HALF, HALF)
         return send(grads.at[kind, slot, :, at], mail.at[kind, to, :, at], device)
 
@@ -343,7 +344,7 @@
         total = own_rows[:, cols].astype(F32) + total.astype(F32)
         for j in range(3):
             total += others[turn, j].astype(F32)
-        out_ref[:, cols] = total.astype(BF16)
+        out_rows[:, cols] = total.astype(BF16)
 
     far, cores, legs = [], [], []
 
@@ -429,51 +430,86 @@
     gain_last = send(gain_half, gain_halves.at[core], sibling)
     gain_halves[core] = gain_half[...]
 
-    outputs = (grad_up_ref, grad_down_ref)
-    for part in range(3):
+    stores = [pltpu.make_async_copy(out_rows, out_ref, local_sem.at[0])]
+    stores[0].start()
+
+    def store(src, dst):
+        stores.append(pltpu.make_async_copy(src, dst, store_sem.at[len(stores) - 1]))
+        stores[-1].start()
+
+    for copy in direct[2]:
+        copy.wait_recv()
+    for kind in range(2):
+        total = grad_tails[kind, 0].astype(F32) + mail_tails[kind, 0].astype(F32)
+        grad_tails[kind, 0] = total.astype(BF16)
+        store(grad_tails.at[kind, 0], sum_tail_ref.at[kind])
+    gain_last.wait()
+    for at in range(2):
+        cols = pl.ds(at * HALF, HALF)
+        gain_out_ref[:, cols] = gain_halves[at] / gain_ref[:, cols]
+    for part in range(2):
         for copy in (*direct[part], *last_leg[part]):
             copy.wait_recv()
-        if part == 2:
-            gain_last.wait()
-            for at in range(2):
-                cols = pl.ds(at * HALF, HALF)
-                gain_out_ref[:, cols] = gain_halves[at] / gain_ref[:, cols]
-            for kind, ref in enumerate(outputs):
-                fourths = []
-                for at in range(3):
-                    cols = fourth_of(at)
-                    total = grad_tails[kind, 0, :, cols].astype(F32)
-                    total += mail_tails[kind, 0, :, cols].astype(F32)
-                    total += mail_tails[kind, 2, :, cols].astype(F32)
-                    fourths.append(total)
-                for at, rows in enumerate(unpack(fourths)):
-                    ref[MAIN:OWN, fourth_of(at)] = rows[0 : OWN - MAIN].astype(BF16)
-            continue
 
         def finish(step, _):
             cols = columns(step, 512, part * HALF)
-            for kind, ref in enumerate(outputs):
+            for kind in range(2):
                 total = grads[kind, 0, :, cols].astype(F32)
                 total += mail[kind, 0, :, cols].astype(F32)
                 total += mail[kind, 2, :, cols].astype(F32)
-                ref[0:MAIN, cols] = total.astype(BF16)
+                grads[kind, 0, :, cols] = total.astype(BF16)
             return 0
 
         lax.fori_loop(0, HALF // 512, finish, 0)
+        for kind in range(2):
+            at = pl.ds(part * HALF, HALF)
+            store(grads.at[kind, 0, :, at], sum_ref.at[kind, :, at])
+    for copy in last_leg[2]:
+        copy.wait_recv()
+    for copy in stores:
+        copy.wait()
 
     for copies in (up_right, down_left, down_right, up_left, up_relay, down_relay, cores, *direct, *far, *last_leg):
         for copy in copies:
             copy.wait_send()
 
 
-def copy_kernel(*refs):
-    sources, targets, held, sems = refs[:4], refs[4:8], refs[8:12], refs[12]
-    loads = [pltpu.make_async_copy(sources[i], held[i], sems.at[0, i]) for i in range(4)]
-    stores = [pltpu.make_async_copy(held[i], targets[i], sems.at[1, i]) for i in range(4)]
-    for load in loads:
-        load.start()
-    for load, store in zip(loads, stores):
-        load.wait()
+def closing_kernel(
+    rows_ref, gain_ref, sum_ref, sum_tail_ref, last_tail_ref, out_ref, gain_out_ref, grad_up_ref, grad_down_ref,
+    rows, gain, tails, tail_lasts, result, load_sem, store_sem,
+):
+    loads = []
+
+    def load(src, dst):
+        loads.append(pltpu.make_async_copy(src, dst, load_sem.at[len(loads)]))
+        loads[-1].start()
+        return loads[-1]
+
+    small = [load(sum_tail_ref, tails), load(last_tail_ref, tail_lasts)]
+    pieces = [(kind, pl.ds(part * HALF, HALF)) for kind in range(2) for part in range(2)]
+    large = [load(sum_ref.at[kind, :, at], result.at[kind, pl.ds(0, MAIN), at]) for kind, at in pieces]
+    copies = [load(rows_ref, rows), load(gain_ref, gain)]
+    stores = [
+        pltpu.make_async_copy(rows, out_ref, store_sem.at[0]),
+        pltpu.make_async_copy(gain, gain_out_ref, store_sem.at[1]),
+    ]
+    for index, (kind, at) in enumerate(pieces):
+        target = (grad_up_ref, grad_down_ref)[kind].at[:, at]
+        stores.append(pltpu.make_async_copy(result.at[kind, :, at], target, store_sem.at[2 + index]))
+    for copy in small:
+        copy.wait()
+    for kind in range(2):
+        fourths = []
+        for at in range(3):
+            cols = pl.ds(at * FOURTH, FOURTH)
+            fourths.append(tails[kind, :, cols].astype(F32) + tail_lasts[kind, :, cols].astype(F32))
+        for at, part in enumerate(unpack(fourths)):
+            result[kind, MAIN:OWN, pl.ds(at * FOURTH, FOURTH)] = part[0 : OWN - MAIN].astype(BF16)
+    for copy, store in zip(large, stores[2:]):
+        copy.wait()
+        store.start()
+    for copy, store in zip(copies, stores):
+        copy.wait()
         store.start()
     for store in stores:
         store.wait()
@@ -485,17 +521,14 @@
 def body(tokens, cotangent, gain, up_weight, down_weight):
     vmem, anywhere = pl.BlockSpec(memory_space=pltpu.VMEM), pl.BlockSpec(memory_space=pl.ANY)
     rows = (1, 4, 2, 2, 32, D)
-    results = (
-        jax.ShapeDtypeStruct((32, D), BF16),
-        jax.ShapeDtypeStruct((1, D), F32),
-        jax.ShapeDtypeStruct((OWN, D), BF16),
-        jax.ShapeDtypeStruct((OWN, D), BF16),
-    )
+    main, tail = jax.ShapeDtypeStruct((2, MAIN, D), BF16), jax.ShapeDtypeStruct((2, 16, TAIL), BF16)
+    out_shape, gain_shape = jax.ShapeDtypeStruct((32, D), BF16), jax.ShapeDtypeStruct((1, D), F32)
+    grad_shape = jax.ShapeDtypeStruct((OWN, D), BF16)
     parts = pl.pallas_call(
         kernel,
-        out_shape=results,
+        out_shape=(out_shape, gain_shape, main, tail, tail),
         in_specs=[anywhere, anywhere, vmem, anywhere, anywhere],
-        out_specs=(vmem, vmem, vmem, vmem),
+        out_specs=(anywhere, vmem, anywhere, anywhere, anywhere),
         scratch_shapes=[
             pltpu.VMEM((2, OWN, D), BF16),
             pltpu.VMEM((2, 4, 2, 2, 32, D), BF16),
@@ -509,11 +542,12 @@
             pltpu.VMEM((2, 4, MAIN, D), BF16),
             pltpu.VMEM((2, 4, 16, TAIL), BF16),
             pltpu.VMEM((2, 3, MAIN, D), BF16),
-            pltpu.VMEM((2, 3, 16, TAIL), BF16),
+            pltpu.VMEM((2, 2, 16, TAIL), BF16),
             pltpu.VMEM((2, 3, 4, 32, FOURTH), BF16),
             pltpu.VMEM((2, 3, 2, 2, 32, FOURTH), BF16),
             pltpu.VMEM((2, 3, 32, FOURTH), BF16),
             pltpu.VMEM((2, 3, 32, FOURTH), BF16),
+            pltpu.VMEM((32, D), BF16),
             pltpu.VMEM((32, D), BF16),
             pltpu.VMEM((8, D), F32),
             pltpu.VMEM((1, D), F32),
@@ -524,16 +558,26 @@
             pltpu.SemaphoreType.DMA((COPIES,)),
             pltpu.SemaphoreType.DMA((COPIES,)),
             pltpu.SemaphoreType.DMA((5,)),
+            pltpu.SemaphoreType.DMA((6,)),
             pltpu.SemaphoreType.REGULAR,
         ],
         compiler_params=pltpu.CompilerParams(collective_id=0, has_side_effects=True, vmem_limit_bytes=63 * 2**20),
     )(tokens.reshape(rows), cotangent.reshape(rows), gain[None], up_weight, down_weight)
     out, gain_out, grad_up, grad_down = pl.pallas_call(
-        copy_kernel,
-        out_shape=results,
-        in_specs=[anywhere] * 4,
+        closing_kernel,
+        out_shape=(out_shape, gain_shape, grad_shape, grad_shape),
+        in_specs=[anywhere] * 5,
         out_specs=(anywhere,) * 4,
-        scratch_shapes=[pltpu.VMEM(part.shape, part.dtype) for part in results] + [pltpu.SemaphoreType.DMA((2, 4))],
+        scratch_shapes=[
+            pltpu.VMEM((32, D), BF16),
+            pltpu.VMEM((1, D), F32),
+            pltpu.VMEM((2, 16, TAIL), BF16),
+            pltpu.VMEM((2, 16, TAIL), BF16),
+            pltpu.VMEM((2, OWN, D), BF16),
+            pltpu.SemaphoreType.DMA((8,)),
+            pltpu.SemaphoreType.DMA((6,)),
+        ],
+        compiler_params=pltpu.CompilerParams(vmem_limit_bytes=63 * 2**20),
     )(*parts)
     return (out[None], gain_out[0], grad_up, grad_down)
 

time: 158 us -> 158 us (level)
  no operation moved by 1% of the time
where the time goes in v4:
time: 158 us
  Pallas kernels  157 us (99%)
    pallas_call x1, Pallas kernels, body(): pl.pallas_call(kernel, out_shape=(out_shape, gain_shape, main, tail, tail...  154 us

profile of v4, /device:TPU:0, one launch (start us, length us, event | category | flops | bytes accessed | tf_op | source)
XLA Modules:
  0.0 157.7 jit_solution(4083606614540119663)
XLA Ops:
  0.6 154.0 %shard_map.84 = (bf16[32,5120]{1,0:T(8,128)(2,1)}, f32[1,5120]{1,0:T(1,128)}, bf16[2,96,5120]{2,1,0:T(8,128)(2,1)}, bf16[2,16,3840]{2,1,0:T(8,128)(2,1)}, bf16[2,16,3840]{2,1,0:T(8,128)(2,1)}) custom-call(bf16[1,4,2,2,32,5120]{5,4,3,2,1,0:T(8,128)(2,1)} %bitcast.5, bf16[1,4,2,2,32,5120]{5,4,3,2,1,0:T(8,128)(2,1)} %bitcast.6, f32[1,5120]{1,0:T(1,128)} %bitcast.7, ...), custom_call_target="tpu_custom_call" | custom-call | tf_op jit(solution)/shard_map/pallas_call | solution.py:527
  154.6 2.9 %shard_map.85 = (bf16[32,5120]{1,0:T(8,128)(2,1)}, f32[1,5120]{1,0:T(1,128)}, bf16[108,5120]{1,0:T(8,128)(2,1)}, bf16[108,5120]{1,0:T(8,128)(2,1)}) custom-call(bf16[32,5120]{1,0:T(8,128)(2,1)} %get-tuple-element.13.rows_ref, f32[1,5120]{1,0:T(1,128)} %get-tuple-element.14.gain_ref, bf16[2,96,5120]{2,1,0:T(8,128)(2,1)} %get-tuple-element.15.sum_ref, ...), custom_call_target="tpu_custom_call" | custom-call | tf_op jit(solution)/shard_map/pallas_call | solution.py:566

commit v5 on v4

--- a/solution.py
+++ b/solution.py
@@ -108,7 +108,6 @@
         return send(tails.at[kind, 0], tails.at[kind, to], device)
 
     up_right, down_left = [send_main(0, 2, z_at(1))], [send_main(1, 1, z_at(3))]
-    down_right, up_left = [send_main(1, 2, z_at(1))], [send_main(0, 1, z_at(3))]
 
     for load in loads:
         load.wait()
@@ -121,8 +120,8 @@
             tails[kind, 0, :, fourth_of(at)] = pack(rows, last, at).astype(BF16)
     up_right.append(send_tail(0, 2, z_at(1)))
     down_left.append(send_tail(1, 1, z_at(3)))
-    down_right.append(send_tail(1, 2, z_at(1)))
-    up_left.append(send_tail(0, 1, z_at(3)))
+    down_right = [send_main(1, 2, z_at(1)), send_tail(1, 2, z_at(1))]
+    up_left = [send_main(0, 1, z_at(3)), send_tail(0, 1, z_at(3))]
     for kind in range(2):
         weights[kind, 0, 0:MAIN, :] = own[kind, 0:MAIN, :]
         for slot in range(1, 4):

time: 158 us -> 158 us (level)
  no operation moved by 1% of the time
where the time goes in v5:
time: 158 us
  Pallas kernels  157 us (99%)
    pallas_call x1, Pallas kernels, body(): pl.pallas_call(kernel, out_shape=(out_shape, gain_shape, main, tail, tail...  154 us

profile of v5, /device:TPU:0, one launch (start us, length us, event | category | flops | bytes accessed | tf_op | source)
XLA Modules:
  0.0 157.7 jit_solution(10789102558009718697)
XLA Ops:
  0.6 154.0 %shard_map.84 = (bf16[32,5120]{1,0:T(8,128)(2,1)}, f32[1,5120]{1,0:T(1,128)}, bf16[2,96,5120]{2,1,0:T(8,128)(2,1)}, bf16[2,16,3840]{2,1,0:T(8,128)(2,1)}, bf16[2,16,3840]{2,1,0:T(8,128)(2,1)}) custom-call(bf16[1,4,2,2,32,5120]{5,4,3,2,1,0:T(8,128)(2,1)} %bitcast.5, bf16[1,4,2,2,32,5120]{5,4,3,2,1,0:T(8,128)(2,1)} %bitcast.6, f32[1,5120]{1,0:T(1,128)} %bitcast.7, ...), custom_call_target="tpu_custom_call" | custom-call | tf_op jit(solution)/shard_map/pallas_call | solution.py:526
  154.6 2.9 %shard_map.85 = (bf16[32,5120]{1,0:T(8,128)(2,1)}, f32[1,5120]{1,0:T(1,128)}, bf16[108,5120]{1,0:T(8,128)(2,1)}, bf16[108,5120]{1,0:T(8,128)(2,1)}) custom-call(bf16[32,5120]{1,0:T(8,128)(2,1)} %get-tuple-element.13.rows_ref, f32[1,5120]{1,0:T(1,128)} %get-tuple-element.14.gain_ref, bf16[2,96,5120]{2,1,0:T(8,128)(2,1)} %get-tuple-element.15.sum_ref, ...), custom_call_target="tpu_custom_call" | custom-call | tf_op jit(solution)/shard_map/pallas_call | solution.py:565

commit v6 on v5

--- a/solution.py
+++ b/solution.py
@@ -485,7 +485,7 @@
         return loads[-1]
 
     small = [load(sum_tail_ref, tails), load(last_tail_ref, tail_lasts)]
-    pieces = [(kind, pl.ds(part * HALF, HALF)) for kind in range(2) for part in range(2)]
+    pieces = [(kind, pl.ds(part * FOURTH, FOURTH)) for kind in range(2) for part in range(4)]
     large = [load(sum_ref.at[kind, :, at], result.at[kind, pl.ds(0, MAIN), at]) for kind, at in pieces]
     copies = [load(rows_ref, rows), load(gain_ref, gain)]
     stores = [
@@ -573,8 +573,8 @@
             pltpu.VMEM((2, 16, TAIL), BF16),
             pltpu.VMEM((2, 16, TAIL), BF16),
             pltpu.VMEM((2, OWN, D), BF16),
-            pltpu.SemaphoreType.DMA((8,)),
-            pltpu.SemaphoreType.DMA((6,)),
+            pltpu.SemaphoreType.DMA((12,)),
+            pltpu.SemaphoreType.DMA((10,)),
         ],
         compiler_params=pltpu.CompilerParams(vmem_limit_bytes=63 * 2**20),
     )(*parts)

time: 158 us -> 158 us (level)
  no operation moved by 1% of the time
where the time goes in v6:
time: 158 us
  Pallas kernels  157 us (99%)
    pallas_call x1, Pallas kernels, body(): pl.pallas_call(kernel, out_shape=(out_shape, gain_shape, main, tail, tail...  154 us

profile of v6, /device:TPU:0, one launch (start us, length us, event | category | flops | bytes accessed | tf_op | source)
XLA Modules:
  0.0 157.7 jit_solution(10654583569654453828)
XLA Ops:
  0.6 154.0 %shard_map.84 = (bf16[32,5120]{1,0:T(8,128)(2,1)}, f32[1,5120]{1,0:T(1,128)}, bf16[2,96,5120]{2,1,0:T(8,128)(2,1)}, bf16[2,16,3840]{2,1,0:T(8,128)(2,1)}, bf16[2,16,3840]{2,1,0:T(8,128)(2,1)}) custom-call(bf16[1,4,2,2,32,5120]{5,4,3,2,1,0:T(8,128)(2,1)} %bitcast.5, bf16[1,4,2,2,32,5120]{5,4,3,2,1,0:T(8,128)(2,1)} %bitcast.6, f32[1,5120]{1,0:T(1,128)} %bitcast.7, ...), custom_call_target="tpu_custom_call" | custom-call | tf_op jit(solution)/shard_map/pallas_call | solution.py:526
  154.6 2.9 %shard_map.85 = (bf16[32,5120]{1,0:T(8,128)(2,1)}, f32[1,5120]{1,0:T(1,128)}, bf16[108,5120]{1,0:T(8,128)(2,1)}, bf16[108,5120]{1,0:T(8,128)(2,1)}) custom-call(bf16[32,5120]{1,0:T(8,128)(2,1)} %get-tuple-element.13.rows_ref, f32[1,5120]{1,0:T(1,128)} %get-tuple-element.14.gain_ref, bf16[2,96,5120]{2,1,0:T(8,128)(2,1)} %get-tuple-element.15.sum_ref, ...), custom_call_target="tpu_custom_call" | custom-call | tf_op jit(solution)/shard_map/pallas_call | solution.py:565
